TPU v7x, 32 devices: a whole 2x2x4 slice. The times are simulated.
32 devices in a mesh: parts: 2 (over x), cols: 16 (over z, y, core).
Axes of the slice: x: 2, y: 2, z: 4, core: 2. Of those that a mesh axis runs over, the one named last changes fastest.
Arguments:
- activations: bfloat16 [4096, 14336], P('parts', 'cols'), parts along dimension 0
- out_grads: bfloat16 [4096, 4096], P(('parts', 'cols')), parts along dimension 0
- queries: bfloat16 [4, 14336, 4096], P('parts', 'cols'), parts along dimension 0
- lengths: int32 [4], P('parts'), parts along dimension 0, may hold values from 256 to 1024, as said below
Outputs:
- influence: float32 [2, 4096], P(None, ('parts', 'cols')), parts along dimension 1
There are 2 independent parts, one for each index of `parts`. A program takes and returns all parts, laid end to end along the dimension named above; each array names one. Nothing has to cross between parts.
Inputs may be any that keep to these rules, and one draw needn't show every extreme that they name: `lengths`: at least one sequence has the full length 1024.
All inputs are finite; a program needn't handle non-finite values.
Results may differ from a plain program's by a relative error of at most 0.0003.
Values may be sent and summed in bfloat16 or wider, within the bound.
A program may use at most 128 MiB of HBM per device.

v0:
```python
import math

import jax
import jax.numpy as jnp
from jax import lax
from jax.sharding import PartitionSpec as P

D = 4096
FF = 14336
LEN = 1024


epsilon = 1e-06


def local(activations, out_grads, queries, lengths):
    tok_dev = out_grads.shape[0]
    query_sq = jnp.sum(jnp.square(queries.astype(jnp.float32)), axis=(1, 2))
    gathered = lax.all_gather(out_grads, "cols", axis=0, tiled=True)
    projected = jnp.einsum("rd,qfd->qrf", gathered, queries, preferred_element_type=jnp.float32)
    partials = jnp.sum(projected * activations.astype(jnp.float32)[None], axis=2)
    act_sq = jnp.sum(jnp.square(activations.astype(jnp.float32)), axis=1)[None, :]
    own_first = lax.axis_index("cols") * tok_dev
    total_scores, total_act, query_total = lax.psum((partials, act_sq, query_sq), "cols")
    own_scores = lax.dynamic_slice_in_dim(total_scores, own_first, tok_dev, 1)
    own_act = lax.dynamic_slice_in_dim(total_act, own_first, tok_dev, 1)
    query_rms = jnp.sqrt(query_total / (FF * D) + epsilon)
    act_rms = jnp.sqrt(own_act[0] / FF + epsilon)
    grad_rms = jnp.sqrt(jnp.sum(jnp.square(out_grads.astype(jnp.float32)), axis=1) / D + epsilon)
    positions = own_first + jnp.arange(tok_dev, dtype=jnp.int32)
    seq_ids = positions // LEN
    owner_match = seq_ids[:, None] == jnp.arange(lengths.shape[0], dtype=jnp.int32)[None, :]
    seq_limit = jnp.sum(jnp.where(owner_match, lengths[None, :], 0), axis=1)
    keep_mask = positions % LEN < seq_limit
    denominator = query_rms[:, None] * act_rms[None, :] * grad_rms[None, :] * math.sqrt(FF * D)
    return jnp.where(keep_mask[None, :], own_scores / denominator, jnp.float32(0.0))


def solution(mesh):
    in_specs = (
        P("parts", "cols"),
        P(("parts", "cols"), None),
        P("parts", "cols", None),
        P("parts"),
    )
    out_specs = P(None, ("parts", "cols"))
    return jax.shard_map(local, mesh=mesh, in_specs=in_specs, out_specs=out_specs, check_vma=False)
```

profile of v0, /device:TPU:0, one launch (start us, length us, event | category | flops | bytes accessed | tf_op | source)
XLA Modules:
  0.0 242.5 jit_solution(18367725704054721409)
XLA Ops:
  6.5 0.0 all-gather.2.cloned.1.call-start
  6.5 0.7 all-gather.2.cloned.1.call-update
  7.3 6.6 %copy.6 = f32[2048,896]{0,1:T(8,128)} copy(bf16[2048,896]{1,0:T(8,128)(2,1)} %param.4) | data formatting | bytes 11010048 | tf_op jit(solution)/shard_map/convert_element_type | solution.py:21
  13.8 0.7 fusion.5
  14.6 1.5 multiply_reduce_fusion.2
  16.1 2.8 %multiply_reduce_fusion.1 = f32[2048]{0:T(1024)S(1)} fusion(bf16[2048,896]{1,0:T(8,128)(2,1)} %param.4), kind=kLoop, calls=%fused_computation.5 | loop fusion | flops 5502976 | bytes 3678208 | tf_op jit(solution)/shard_map/reduce_sum | solution.py:22
  19.0 10.0 %multiply_reduce_fusion = f32[2]{0:T(128)S(1)} fusion(bf16[2,896,4096]{2,1,0:T(8,128)(2,1)} %param.6), kind=kLoop, calls=%fused_computation | loop fusion | flops 22020094 | bytes 14680072 | tf_op jit(solution)/shard_map/reduce_sum | solution.py:18
  28.9 110.2 %all-gather.2.cloned.1.call-done = bf16[2048,4096]{1,0:T(8,128)(2,1)} async-done(((bf16[128,4096]{1,0:T(8,128)(2,1)}), bf16[2048,4096]{1,0:T(8,128)(2,1)}) %all-gather.2.cloned.1.call-update) | async-done | bytes 16777232 | tf_op jit(solution)/shard_map/all_gather | solution.py:19
  139.1 37.2 %fusion.2 = f32[2,2048]{1,0:T(2,128)S(1)} fusion(f32[2048,896]{0,1:T(8,128)} %copy.6, bf16[2,896,4096]{2,1,0:T(8,128)(2,1)} %param.6, bf16[2048,4096]{1,0:T(8,128)(2,1)} %all-gather.2.cloned.1.call-done), kind=kOutput, calls=%fused_computation.4 | convolution fusion | flops 30072107008 | bytes 38813696 | tf_op jit(solution)/shard_map/rd,qfd->qrf/dot_general | solution.py:20
  176.3 58.7 %all-reduce = (f32[2,2048]{1,0:T(2,128)S(1)}, f32[1,2048]{1,0:T(1,128)S(1)}, f32[2]{0:T(128)S(1)}) all-reduce(f32[2,2048]{1,0:T(2,128)S(1)} %fusion.2, f32[1,2048]{1,0:T(1,128)S(1)} %bitcast.13, f32[2]{0:T(128)S(1)} %multiply_reduce_fusion), channel_id=1, replica_groups=mesh['parts'=2,'cols'=16] {'cols'}, use_global_device_ids=true, to_apply=%region_2.0 | all-reduce | flops 6146 | bytes 49168 | tf_op jit(solution)/shard_map/psum | solution.py:24
  235.0 0.6 fusion.6
  (5 shorter events, 0.0 us)
Async XLA Ops:
  6.5 132.6 %all-gather.2.cloned.1.call-start = ((), (), s32[]{:S(2)}) async-start(), calls=%async_computation | async-start | bytes 17825792 | tf_op jit(solution)/shard_map/all_gather | solution.py:19
Sparse Core Ops, SparseCore 0:
  9.5 129.5 all-gather.1
where the time goes:
time: 243 us; the launch traced here: 242 us
  waiting for transfers between devices  111 us (46%)
  blocking collectives  58.7 us (24%)
  matrix products  37.2 us (15%)
  other arithmetic  15.7 us (6%)
  between operations  13.4 us (6%)
  local copies, waits for them, and re-layouts  6.57 us (3%)
    all_gather x1, waiting for transfers between devices, local(): gathered = lax.all_gather(out_grads, 'cols', axis=0, tiled=True)  110 us
    psum x1, blocking collectives, local(): lax.psum((partials, act_sq, query_sq), 'cols')  58.7 us
    dot_general x1, matrix products, local(): jnp.einsum('rd,qfd->qrf', gathered, queries, preferred_element_type=jnp.f...  37.2 us
    reduce_sum x1, other arithmetic, local(): query_sq = jnp.sum(jnp.square(queries.astype(jnp.float32)), axis=(1, 2))  9.96 us
    convert_element_type x1, local copies, waits for them, and re-layouts, local(): activations.astype(jnp.float32)[None]  6.57 us
  transfers between devices with their start and end apart: 1, of which 1 were waited for; matrix products, arithmetic and copies ran while one was open for 9% of the time, Pallas kernels for 0%

commit v1 on v0

v1 whole, which is shorter than its diff:
```python
import functools
import math

import jax
import jax.numpy as jnp
from jax import lax
from jax.experimental import pallas as pl
from jax.experimental.pallas import tpu as pltpu
from jax.sharding import PartitionSpec as P

LEN = 1024
SUBS = 4
LANES = 128
MESH = pl.DeviceIdType.MESH

epsilon = 1e-06


def kernel(sizes, og, act, qry, lens, out, G, A, Q, acc, qtile, gsq, res, parts,
           recv, s_in, s_out, s_y, s_sib, r_send, r_recv, lsem):
    ncols, ff, d_model, seqs = sizes
    sub_rows = og.shape[1]
    half_rows = 2 * sub_rows
    tok = SUBS * sub_rows
    me = lax.axis_index("cols")
    z, y, c = lax.div(me, 4), lax.rem(lax.div(me, 2), 2), lax.rem(me, 2)
    hi = lax.div(z, 2)
    d = 1 - 2 * hi
    m = lax.rem(z + hi, 2)
    edge, mid = m == 0, m == 1
    own = 2 * z + y

    def dev(zz, yy, cc):
        return 4 * zz + 2 * yy + cc

    sib, ydev = dev(z, y, 1 - c), dev(z, 1 - y, c)
    indev, outdev = dev(z + d, y, c), dev(z - d, y, c)

    def copy(src, p, s, target, sem):
        return pltpu.make_async_remote_copy(
            src_ref=src, dst_ref=G.at[p, c, s], send_sem=sem, recv_sem=recv.at[2 * p + c, s],
            device_id={"cols": target}, device_id_type=MESH)

    def await_chunk(p, cc, s):
        pltpu.make_async_remote_copy(
            src_ref=G.at[p, cc, s], dst_ref=G.at[p, cc, s], send_sem=s_sib.at[0, 0],
            recv_sem=recv.at[2 * p + cc, s], device_id={"cols": sib}, device_id_type=MESH).wait_recv()

    loads = [pltpu.make_async_copy(og, G.at[own, c], lsem.at[0]),
             pltpu.make_async_copy(qry.at[0], Q.at[0], lsem.at[1]),
             pltpu.make_async_copy(qry.at[1], Q.at[1], lsem.at[2]),
             pltpu.make_async_copy(act, A, lsem.at[3])]
    for load in loads:
        load.start()

    barrier = pltpu.get_barrier_semaphore()

    def greet(k, _):
        pl.semaphore_signal(barrier, inc=1, device_id={"cols": lax.rem(me + k, ncols)}, device_id_type=MESH)
        return 0

    lax.fori_loop(1, ncols, greet, 0)
    pl.semaphore_wait(barrier, ncols - 1)

    for s in range(SUBS):
        copy(og.at[s], own, s, ydev, s_y.at[s]).start()
        copy(og.at[s], own, s, indev, s_in.at[s]).start()

        @pl.when(mid)
        def _():
            copy(og.at[s], own, s, outdev, s_out.at[s]).start()

        copy(og.at[s], own, s, sib, s_sib.at[own, s]).start()

    for load in loads:
        load.wait()

    row = lax.broadcasted_iota(jnp.int32, (8, LANES), 0)
    qbase = jnp.zeros((8, LANES), jnp.float32)
    for q in range(2):
        def add_squares(r, total):
            x = Q[q, pl.ds(pl.multiple_of(r * 16, 16), 16), :].astype(jnp.float32)
            x = x * x
            parts_ = [x[:, k * LANES:(k + 1) * LANES] for k in range(d_model // LANES)]
            while len(parts_) > 1:
                parts_ = [a + b for a, b in zip(parts_[::2], parts_[1::2])]
            return total + parts_[0]

        total = lax.fori_loop(0, Q.shape[1] // 16, add_squares, jnp.zeros((16, LANES), jnp.float32))
        qbase = jnp.where(row == 3 + q, jnp.sum(total), qbase)
    qtile[...] = qbase
    for s in range(SUBS):
        x = jnp.zeros((sub_rows, LANES), jnp.float32)
        for k in range(d_model // LANES):
            g = G[own, c, s, :, pl.ds(k * LANES, LANES)].astype(jnp.float32)
            x = x + g * g
        gsq[s * sub_rows:(s + 1) * sub_rows, :] = x

    def send_result(p, h, tile):
        res[2 * p + h] = tile
        for cc in range(2):
            target = 2 * p + cc

            @pl.when(target == me)
            def _():
                parts[me, h] = tile

            @pl.when(target != me)
            def _():
                pltpu.make_async_remote_copy(
                    src_ref=res.at[2 * p + h], dst_ref=parts.at[me, h], send_sem=r_send.at[2 * p + h, cc],
                    recv_sem=r_recv.at[me, h], device_id={"cols": target}, device_id_type=MESH).start()

    def compute(pa, ha, pb, hb):
        for p, h in ((pa, ha), (pb, hb)):
            for s in range(2):
                await_chunk(p, 1 - c, 2 * h + s)
        acc[...] = jnp.zeros_like(acc)

        def tile_step(i, _):
            cols = pl.ds(pl.multiple_of(i * LANES, LANES), LANES)
            lhs = jnp.concatenate([
                G[pa, :, pl.ds(2 * ha, 2)].reshape(2 * half_rows, d_model),
                G[pb, :, pl.ds(2 * hb, 2)].reshape(2 * half_rows, d_model)], axis=0)
            rhs = Q[:, cols, :].reshape(2 * LANES, d_model)
            pr = lax.dot_general(lhs, rhs, (((1,), (1,)), ((), ())), preferred_element_type=jnp.float32)
            a = jnp.concatenate([
                A[pa, :, pl.ds(2 * ha, 2), :, cols].reshape(2 * half_rows, LANES),
                A[pb, :, pl.ds(2 * hb, 2), :, cols].reshape(2 * half_rows, LANES)], axis=0).astype(jnp.float32)
            acc[0] += pr[:, :LANES] * a
            acc[1] += pr[:, LANES:] * a
            acc[2] += a * a
            return 0

        lax.fori_loop(0, Q.shape[1] // LANES, tile_step, 0)
        for j, (p, h) in enumerate(((pa, ha), (pb, hb))):
            tile = qtile[...]
            for k in range(3):
                block = acc[k, j * 2 * half_rows:(j + 1) * 2 * half_rows, :]
                tile = jnp.where(row == k, jnp.sum(block.T, axis=0, keepdims=True), tile)
            send_result(p, h, tile)

    z1, z2, z3, zo = z + d, z + 2 * d, z + 3 * d, z - d
    other = 1 - y

    def pick(a, b):
        return jnp.where(edge, a, b)

    def step(u, _):
        is_unit = functools.reduce(jnp.logical_or, [u == t for t in UNIT_STEPS])
        unit = sum([(u >= t).astype(jnp.int32) for t in UNIT_STEPS]) - 1

        @pl.when(is_unit)
        def _():
            pa, pb = own, own
            split = jnp.logical_and(edge, unit >= 6)
            table = (
                (own, own),
                (2 * z1 + y,) * 2,
                (2 * z + other,) * 2,
                (pick(2 * z2 + y, 2 * zo + y),) * 2,
                (pick(2 * z2 + other, 2 * zo + other),) * 2,
                (pick(2 * z3 + y, 2 * z2 + y),) * 2,
                (2 * z1 + other, pick(2 * z3 + other, 2 * z1 + other)),
                (pick(2 * z1 + other, 2 * z2 + other), pick(2 * z3 + other, 2 * z2 + other)),
            )
            for t, (a, b) in enumerate(table):
                pa = jnp.where(unit == t, a, pa)
                pb = jnp.where(unit == t, b, pb)
            ha = jnp.where(split, unit - 6, 0)
            hb = jnp.where(split, unit - 6, 1)
            compute(pa, ha, pb, hb)

        @pl.when(jnp.logical_and(u < 14, jnp.logical_or(edge, u < 8)))
        def _():
            own_line = u < 12
            p = jnp.where(own_line, 2 * (z + d * (1 + lax.div(u, 4))) + y, 2 * z1 + other)
            s = jnp.where(own_line, lax.rem(u, 4), u - 10)
            await_chunk(p, c, s)

            @pl.when(mid)
            def _():
                copy(G.at[p, c, s], p, s, outdev, s_out.at[4 + u]).start()

            skip = jnp.logical_and(edge, jnp.logical_or(jnp.logical_or(u == 2, u == 3), u >= 12))

            @pl.when(jnp.logical_not(skip))
            def _():
                k = pick(jnp.where(u < 2, 4 + u, u + 2), jnp.where(u < 2, 4 + 2 * u, u + 6))
                copy(G.at[p, c, s], p, s, ydev, s_y.at[k]).start()

            copy(G.at[p, c, s], p, s, sib, s_sib.at[p, s]).start()

        @pl.when(jnp.logical_and(mid, u < 6))
        def _():
            own_line = u < 4
            p = jnp.where(own_line, 2 * zo + y, 2 * zo + other)
            s = jnp.where(own_line, u, u - 2)
            await_chunk(p, c, s)

            @pl.when(own_line)
            def _():
                copy(G.at[p, c, s], p, s, indev, s_in.at[4 + u]).start()

            @pl.when(u < 2)
            def _():
                copy(G.at[p, c, s], p, s, ydev, s_y.at[5 + 2 * u]).start()

            copy(G.at[p, c, s], p, s, sib, s_sib.at[p, s]).start()

        @pl.when(u < 14)
        def _():
            ne = jnp.where(u < 6, u - 4, u - 2)
            ze, se = z + d * (1 + lax.div(ne, 4)), lax.rem(ne, 4)
            early = u < 8
            from_out = jnp.logical_and(early, lax.rem(u, 2) == 1)
            nm = jnp.where(early, lax.div(u - 4, 2), u - 6)
            zm, sm = jnp.where(from_out, zo, z + d * (1 + lax.div(nm, 4))), lax.rem(nm, 4)
            first = u < 4
            p = 2 * jnp.where(first, z, pick(ze, zm)) + other
            s = jnp.where(first, u, pick(se, sm))
            await_chunk(p, c, s)
            copy(G.at[p, c, s], p, s, sib, s_sib.at[p, s]).start()

            @pl.when(jnp.logical_and(edge, jnp.logical_or(u == 2, u == 3)))
            def _():
                copy(G.at[p, c, s], p, s, indev, s_in.at[2 + u]).start()

        @pl.when(jnp.logical_and(mid, jnp.logical_or(u == 8, u == 9)))
        def _():
            p, s = 2 * z + other, u - 6
            copy(G.at[p, c, s], p, s, outdev, s_out.at[4 + u]).start()

        return 0

    lax.fori_loop(0, 15, step, 0)

    def settle(sem):
        copy(og.at[0], own, 0, sib, sem).wait_send()

    def settle_y(k, _):
        settle(s_y.at[k])

        @pl.when(mid)
        def _():
            settle(s_out.at[k])

        @pl.when(k < pick(6, 8))
        def _():
            settle(s_in.at[k])

        return 0

    lax.fori_loop(0, 14, settle_y, 0)

    def settle_sib(p, _):
        for s in range(SUBS):
            settle(s_sib.at[p, s])
        return 0

    lax.fori_loop(0, ncols // 2, settle_sib, 0)

    def result(src, h, cc_sem):
        return pltpu.make_async_remote_copy(
            src_ref=res.at[0], dst_ref=parts.at[src, h], send_sem=cc_sem,
            recv_sem=r_recv.at[src, h], device_id={"cols": sib}, device_id_type=MESH)

    def gather_results(k, _):
        src = lax.rem(me + k, ncols)
        for h in range(2):
            result(src, h, r_send.at[0, 0]).wait_recv()
            p, cc = lax.div(src, 2), lax.rem(src, 2)
            result(src, h, r_send.at[2 * p + h, cc]).wait_send()
        return 0

    lax.fori_loop(1, ncols, gather_results, 0)

    t0, t1 = parts[0, 0], parts[0, 1]
    for src in range(1, ncols):
        t0, t1 = t0 + parts[src, 0], t1 + parts[src, 1]
    lane = lax.broadcasted_iota(jnp.int32, (1, LANES), 1)
    low = jnp.where(c == 0, t0, jnp.roll(t0, half_rows, axis=1))
    high = jnp.where(c == 0, jnp.roll(t1, half_rows, axis=1), t1)
    full = jnp.where(lane < half_rows, low, high)
    query_rms = jnp.sqrt(full[3:5] / (ff * d_model) + epsilon)
    act_rms = jnp.sqrt(full[2:3] / ff + epsilon)
    grad_rms = jnp.sqrt(jnp.sum(gsq[...].T, axis=0, keepdims=True) / d_model + epsilon)
    positions = me * tok + lane
    seq_ids = lax.div(positions, LEN)
    limit = jnp.zeros((1, LANES), jnp.int32)
    for q in range(seqs):
        limit = jnp.where(seq_ids == q, lens[q], limit)
    keep = lax.rem(positions, LEN) < limit
    influence = full[0:2] / (query_rms * act_rms * grad_rms * math.sqrt(ff * d_model))
    out[...] = jnp.where(keep, influence, 0.0)


UNIT_STEPS = (0, 4, 5, 8, 10, 12, 13, 14)


def fused(ncols, activations, out_grads, queries, lengths):
    tok, d_model = out_grads.shape
    nq, ff_dev, _ = queries.shape
    pairs, sub = ncols // 2, tok // SUBS
    sizes = (ncols, ff_dev * ncols, d_model, lengths.shape[0])
    tokens = ncols * tok
    dma = pltpu.SemaphoreType.DMA
    return pl.pallas_call(
        functools.partial(kernel, sizes),
        out_shape=jax.ShapeDtypeStruct((nq, tok), jnp.float32),
        in_specs=[pl.BlockSpec(memory_space=pl.ANY)] * 3 + [pl.BlockSpec(memory_space=pltpu.SMEM)],
        out_specs=pl.BlockSpec(memory_space=pltpu.VMEM),
        scratch_shapes=[
            pltpu.VMEM((pairs, 2, SUBS, sub, d_model), jnp.bfloat16),
            pltpu.VMEM((pairs, 2, SUBS, sub, ff_dev), jnp.bfloat16),
            pltpu.VMEM((nq, ff_dev, d_model), jnp.bfloat16),
            pltpu.VMEM((3, 2 * tok, LANES), jnp.float32),
            pltpu.VMEM((8, LANES), jnp.float32),
            pltpu.VMEM((tok, LANES), jnp.float32),
            pltpu.VMEM((2 * pairs, 8, LANES), jnp.float32),
            pltpu.VMEM((ncols, 2, 8, LANES), jnp.float32),
            dma((ncols, SUBS)), dma((8,)), dma((14,)), dma((14,)), dma((pairs, SUBS)),
            dma((2 * pairs, 2)), dma((ncols, 2)), dma((4,)),
        ],
        compiler_params=pltpu.CompilerParams(
            collective_id=0, has_side_effects=True, vmem_limit_bytes=54 * 2**20),
        cost_estimate=pl.CostEstimate(
            flops=2 * nq * tokens * ff_dev * d_model, transcendentals=0,
            bytes_accessed=2 * (nq * ff_dev * d_model + tokens * ff_dev + tok * d_model)),
    )(
        out_grads.reshape(SUBS, sub, d_model),
        activations.reshape(pairs, 2, SUBS, sub, ff_dev),
        queries, lengths)


def local(activations, out_grads, queries, lengths):
    tok_dev, d_model = out_grads.shape
    query_sq = jnp.sum(jnp.square(queries.astype(jnp.float32)), axis=(1, 2))
    gathered = lax.all_gather(out_grads, "cols", axis=0, tiled=True)
    projected = jnp.einsum("rd,qfd->qrf", gathered, queries, preferred_element_type=jnp.float32)
    partials = jnp.sum(projected * activations.astype(jnp.float32)[None], axis=2)
    act_sq = jnp.sum(jnp.square(activations.astype(jnp.float32)), axis=1)[None, :]
    own_first = lax.axis_index("cols") * tok_dev
    total_scores, total_act, query_total = lax.psum((partials, act_sq, query_sq), "cols")
    own_scores = lax.dynamic_slice_in_dim(total_scores, own_first, tok_dev, 1)
    own_act = lax.dynamic_slice_in_dim(total_act, own_first, tok_dev, 1)
    ff = queries.shape[1] * lax.axis_size("cols")
    query_rms = jnp.sqrt(query_total / (ff * d_model) + epsilon)
    act_rms = jnp.sqrt(own_act[0] / ff + epsilon)
    grad_rms = jnp.sqrt(jnp.sum(jnp.square(out_grads.astype(jnp.float32)), axis=1) / d_model + epsilon)
    positions = own_first + jnp.arange(tok_dev, dtype=jnp.int32)
    seq_ids = positions // LEN
    owner_match = seq_ids[:, None] == jnp.arange(lengths.shape[0], dtype=jnp.int32)[None, :]
    seq_limit = jnp.sum(jnp.where(owner_match, lengths[None, :], 0), axis=1)
    keep_mask = positions % LEN < seq_limit
    denominator = query_rms[:, None] * act_rms[None, :] * grad_rms[None, :] * math.sqrt(ff * d_model)
    return jnp.where(keep_mask[None, :], own_scores / denominator, jnp.float32(0.0))


def solution(mesh):
    in_specs = (
        P("parts", "cols"),
        P(("parts", "cols"), None),
        P("parts", "cols", None),
        P("parts"),
    )
    out_specs = P(None, ("parts", "cols"))
    ncols = mesh.shape["cols"]
    body = functools.partial(fused, ncols) if ncols == 16 else local
    return jax.shard_map(body, mesh=mesh, in_specs=in_specs, out_specs=out_specs, check_vma=False)
```

time: 243 us -> 103 us (0.42)
  waiting for transfers between devices: 111 us -> 0 us
  Pallas kernels: 0 us -> 102 us
  blocking collectives: 58.7 us -> 0 us
  matrix products: 37.2 us -> 0 us
  other arithmetic: 15.7 us -> 0 us
  between operations: 13.4 us -> 0.01 us
  local copies, waits for them, and re-layouts: 6.57 us -> 1.24 us
    all_gather x1 -> x0, waiting for transfers between devices: 110 us -> none  [local(): gathered = lax.all_gather(out_grads, 'cols', axis=0, tiled=True)]
    pallas_call x0 -> x1, Pallas kernels: none -> 102 us  [fused(): pl.pallas_call(functools.partial(kernel, sizes), out_shape=jax.ShapeDtype...]
    psum x1 -> x0, blocking collectives: 58.7 us -> none  [local(): lax.psum((partials, act_sq, query_sq), 'cols')]
    dot_general x1 -> x0, matrix products: 37.2 us -> none  [local(): jnp.einsum('rd,qfd->qrf', gathered, queries, preferred_element_type=jnp.f...]
    reduce_sum x4 -> x0, other arithmetic: 15 us -> none  [the longest x1 9.96 us: local(): query_sq = jnp.sum(jnp.square(queries.astype(jnp.float32)), axis=(1, 2))]
    convert_element_type x1 -> x0, local copies, waits for them, and re-layouts: 6.57 us -> none  [local(): activations.astype(jnp.float32)[None]]
  transfers between devices with their start and end apart: 1 -> 0, of which waited for: 1 -> 0; matrix products, arithmetic and copies ran while one was open for 9% -> 0% of each run, Pallas kernels for 0% -> 0%
where the time goes in v1:
time: 103 us
  Pallas kernels  102 us (99%)
  local copies, waits for them, and re-layouts  1.24 us (1%)
    pallas_call x1, Pallas kernels, fused(): pl.pallas_call(functools.partial(kernel, sizes), out_shape=jax.ShapeDtype...  102 us

profile of v1, /device:TPU:0, one launch (start us, length us, event | category | flops | bytes accessed | tf_op | source)
XLA Modules:
  0.0 103.1 jit_solution(2163353107729888666)
XLA Ops:
  0.0 101.9 %shard_map.46 = f32[2,128]{1,0:T(2,128)} custom-call(bf16[4,32,4096]{2,1,0:T(8,128)(2,1)} %bitcast.3, bf16[8,2,4,32,896]{4,3,2,1,0:T(8,128)(2,1)} %bitcast.2, bf16[2,896,4096]{2,1,0:T(8,128)(2,1)} %qry.1, s32[2]{0:T(128)} %lens.1), custom_call_target="tpu_custom_call" | custom-call | flops 30064771072 | bytes 19398656 | tf_op jit(solution)/shard_map/pallas_call | solution.py:308
  101.9 1.2 %copy.6 = f32[2,128]{1,0:T(2,128)} copy(f32[2,128]{1,0:T(2,128)} %shard_map.46) | data formatting | bytes 2048

commit v2 on v1

v2 whole, which is shorter than its diff:
```python
import functools
import math

import jax
import jax.numpy as jnp
from jax import lax
from jax.experimental import pallas as pl
from jax.experimental.pallas import tpu as pltpu
from jax.sharding import PartitionSpec as P

LEN = 1024
SUBS = 4
LANES = 128
MESH = pl.DeviceIdType.MESH

epsilon = 1e-06


def kernel(sizes, og, act, qry, lens, out, G, A, AT, Q, acc, asq, qtile, gsq, res, parts,
           recv, s_in, s_out, s_y, s_sib, r_send, r_recv, lsem):
    ncols, ff, d_model, seqs = sizes
    tok = og.shape[0]
    width = d_model // SUBS
    ff_dev = Q.shape[1]
    pairs = ncols // 2
    me = lax.axis_index("cols")
    z, y, c = lax.div(me, 4), lax.rem(lax.div(me, 2), 2), lax.rem(me, 2)
    hi = lax.div(z, 2)
    d = 1 - 2 * hi
    m = lax.rem(z + hi, 2)
    edge, mid = m == 0, m == 1
    own = 2 * z + y

    def dev(zz, yy, cc):
        return 4 * zz + 2 * yy + cc

    sib, ydev = dev(z, y, 1 - c), dev(z, 1 - y, c)
    indev, outdev = dev(z + d, y, c), dev(z - d, y, c)

    def copy(src, p, s, target, sem):
        return pltpu.make_async_remote_copy(
            src_ref=src, dst_ref=G.at[p, c, s], send_sem=sem, recv_sem=recv.at[2 * p + c, s],
            device_id={"cols": target}, device_id_type=MESH)

    def await_chunk(p, cc, s):
        pltpu.make_async_remote_copy(
            src_ref=G.at[p, cc, s], dst_ref=G.at[p, cc, s], send_sem=s_sib.at[0, 0],
            recv_sem=recv.at[2 * p + cc, s], device_id={"cols": sib}, device_id_type=MESH).wait_recv()

    def mine(s):
        return og.at[:, pl.ds(s * width, width)]

    act_load = pltpu.make_async_copy(act, A, lsem.at[0])
    loads = [pltpu.make_async_copy(qry.at[q], Q.at[q], lsem.at[1 + q]) for q in range(2)]
    loads += [pltpu.make_async_copy(mine(s), G.at[own, c, s], lsem.at[3 + s]) for s in range(SUBS)]
    act_load.start()
    for load in loads:
        load.start()

    barrier = pltpu.get_barrier_semaphore()

    def greet(k, _):
        pl.semaphore_signal(barrier, inc=1, device_id={"cols": lax.rem(me + k, ncols)}, device_id_type=MESH)
        return 0

    lax.fori_loop(1, ncols, greet, 0)
    pl.semaphore_wait(barrier, ncols - 1)

    for s in range(SUBS):
        copy(mine(s), own, s, ydev, s_y.at[s]).start()
        copy(mine(s), own, s, indev, s_in.at[s]).start()

        @pl.when(mid)
        def _():
            copy(mine(s), own, s, outdev, s_out.at[s]).start()

        copy(mine(s), own, s, sib, s_sib.at[own, s]).start()

    acc[...] = jnp.zeros_like(acc)
    act_load.wait()

    def turn(p, _):
        total = jnp.zeros((8, 2 * tok), jnp.float32)
        for i in range(ff_dev // LANES):
            x = A[p, :, i * LANES:(i + 1) * LANES].astype(jnp.float32).T
            AT[p, i * LANES:(i + 1) * LANES, :] = x
            total = total + jnp.sum((x * x).reshape(LANES // 8, 8, 2 * tok), axis=0)
        asq[p] = total
        return 0

    lax.fori_loop(0, pairs, turn, 0)
    for load in loads:
        load.wait()

    row = lax.broadcasted_iota(jnp.int32, (8, 2 * tok), 0)
    qbase = jnp.zeros((8, 2 * tok), jnp.float32)
    for q in range(2):
        def add_squares(r, total):
            x = Q[q, pl.ds(pl.multiple_of(r * 16, 16), 16), :].astype(jnp.float32)
            x = x * x
            terms = [x[:, k * LANES:(k + 1) * LANES] for k in range(d_model // LANES)]
            while len(terms) > 1:
                terms = [a + b for a, b in zip(terms[::2], terms[1::2])]
            return total + terms[0]

        total = lax.fori_loop(0, ff_dev // 16, add_squares, jnp.zeros((16, LANES), jnp.float32))
        qbase = jnp.where(row == 3 + q, jnp.sum(total), qbase)
    qtile[...] = qbase
    x = jnp.zeros((tok, LANES), jnp.float32)
    for s in range(SUBS):
        for k in range(width // LANES):
            g = G[own, c, s, :, k * LANES:(k + 1) * LANES].astype(jnp.float32)
            x = x + g * g
    gsq[...] = x

    z1, zo = z + d, z - d
    other = 1 - y

    def inner_chunk(u):
        line = u < 12
        return (jnp.where(line, 2 * (z + d * (1 + lax.div(u, 4))) + y, 2 * z1 + other),
                jnp.where(line, lax.rem(u, 4), u - 10))

    def outer_chunk(u):
        line = u < 4
        return 2 * zo + jnp.where(line, y, other), jnp.where(line, u, u - 2)

    def y_chunk(u):
        ne = jnp.where(u < 6, u - 4, u - 2)
        from_out = jnp.logical_and(u < 8, lax.rem(u, 2) == 1)
        nm = jnp.where(u < 8, lax.div(u - 4, 2), u - 6)
        n = jnp.where(edge, ne, nm)
        zz = jnp.where(jnp.logical_and(mid, from_out), zo, z + d * (1 + lax.div(n, 4)))
        first = u < 4
        return (2 * jnp.where(first, z, zz) + other,
                jnp.where(first, u, lax.rem(n, 4)))

    def has_inner(u):
        return jnp.logical_and(u < 14, jnp.logical_or(edge, u < 8))

    def has_outer(u):
        return jnp.logical_and(mid, u < 6)

    def finish(p):
        tile = qtile[...]
        for k, value in enumerate((acc[p, 0], acc[p, 1], asq[p])):
            tile = jnp.where(row == k, jnp.sum(value, axis=0, keepdims=True), tile)
        for cc in range(2):
            target = 2 * p + cc
            half = tile[:, cc * tok:(cc + 1) * tok]
            res[p, cc] = half

            @pl.when(target == me)
            def _():
                parts[me] = half

            @pl.when(target != me)
            def _():
                pltpu.make_async_remote_copy(
                    src_ref=res.at[p, cc], dst_ref=parts.at[me], send_sem=r_send.at[p, cc],
                    recv_sem=r_recv.at[me], device_id={"cols": target}, device_id_type=MESH).start()

    def multiply(p, s_first, count, last):
        def one(j, _):
            s, q = s_first + lax.div(j, 2), lax.rem(j, 2)

            @pl.when(q == 0)
            def _():
                await_chunk(p, 1 - c, s)

            rhs = G[p, :, s].reshape(2 * tok, width)
            lhs = Q[q, :, pl.ds(pl.multiple_of(s * width, width), width)]
            pr = lax.dot_general(lhs, rhs, (((1,), (1,)), ((), ())), preferred_element_type=jnp.float32)
            acc[p, q] += jnp.sum((pr * AT[p]).reshape(ff_dev // 8, 8, 2 * tok), axis=0)
            return 0

        lax.fori_loop(0, 2 * count, one, 0)

        @pl.when(last)
        def _():
            finish(p)

    def step(u, _):
        def task(t, _):
            v = u - 1
            pi, si = inner_chunk(v)
            po, so = outer_chunk(v)
            py, sy = y_chunk(v)
            start = u == 0
            p = jnp.where(start, own, jnp.where(t == 0, pi, jnp.where(t == 1, po, py)))
            s = jnp.where(start, 0, jnp.where(t == 0, si, jnp.where(t == 1, so, sy)))
            go = jnp.where(t == 0, jnp.logical_or(start, has_inner(v)).astype(jnp.int32),
                           jnp.where(t == 1, jnp.logical_and(u > 0, has_outer(v)).astype(jnp.int32),
                                     (u > 0).astype(jnp.int32)))
            last_in = jnp.logical_or(start, si == 3)
            last_y = jnp.logical_or(sy == 3, jnp.logical_and(mid, v == 7))
            last = jnp.where(t == 0, last_in.astype(jnp.int32),
                             jnp.where(t == 1, (v == 3).astype(jnp.int32), last_y.astype(jnp.int32)))

            @pl.when(go == 1)
            def _():
                multiply(p, s, jnp.where(start, SUBS, 1), last == 1)

            return 0

        lax.fori_loop(0, 3, task, 0)

        @pl.when(has_inner(u))
        def _():
            p, s = inner_chunk(u)
            await_chunk(p, c, s)

            @pl.when(mid)
            def _():
                copy(G.at[p, c, s], p, s, outdev, s_out.at[4 + u]).start()

            skip = jnp.logical_and(edge, jnp.logical_or(jnp.logical_or(u == 2, u == 3), u >= 12))

            @pl.when(jnp.logical_not(skip))
            def _():
                k = jnp.where(edge, jnp.where(u < 2, 4 + u, u + 2), jnp.where(u < 2, 4 + 2 * u, u + 6))
                copy(G.at[p, c, s], p, s, ydev, s_y.at[k]).start()

            copy(G.at[p, c, s], p, s, sib, s_sib.at[p, s]).start()

        @pl.when(has_outer(u))
        def _():
            p, s = outer_chunk(u)
            await_chunk(p, c, s)

            @pl.when(u < 4)
            def _():
                copy(G.at[p, c, s], p, s, indev, s_in.at[4 + u]).start()

            @pl.when(u < 2)
            def _():
                copy(G.at[p, c, s], p, s, ydev, s_y.at[5 + 2 * u]).start()

            copy(G.at[p, c, s], p, s, sib, s_sib.at[p, s]).start()

        @pl.when(u < 14)
        def _():
            p, s = y_chunk(u)
            await_chunk(p, c, s)
            copy(G.at[p, c, s], p, s, sib, s_sib.at[p, s]).start()

            @pl.when(jnp.logical_and(edge, jnp.logical_or(u == 2, u == 3)))
            def _():
                copy(G.at[p, c, s], p, s, indev, s_in.at[2 + u]).start()

        @pl.when(jnp.logical_and(mid, jnp.logical_or(u == 8, u == 9)))
        def _():
            p, s = 2 * z + other, u - 6
            copy(G.at[p, c, s], p, s, outdev, s_out.at[4 + u]).start()

        return 0

    lax.fori_loop(0, 15, step, 0)

    def settle(sem):
        copy(mine(0), own, 0, sib, sem).wait_send()

    def settle_links(k, _):
        settle(s_y.at[k])

        @pl.when(mid)
        def _():
            settle(s_out.at[k])

        @pl.when(k < jnp.where(edge, 6, 8))
        def _():
            settle(s_in.at[k])

        return 0

    lax.fori_loop(0, 14, settle_links, 0)

    def settle_sib(p, _):
        for s in range(SUBS):
            settle(s_sib.at[p, s])
        return 0

    lax.fori_loop(0, pairs, settle_sib, 0)

    def gather_results(k, _):
        src = lax.rem(me + k, ncols)
        p, cc = lax.div(src, 2), lax.rem(src, 2)
        result = pltpu.make_async_remote_copy(
            src_ref=res.at[p, cc], dst_ref=parts.at[src], send_sem=r_send.at[p, cc],
            recv_sem=r_recv.at[src], device_id={"cols": src}, device_id_type=MESH)
        result.wait_recv()
        result.wait_send()
        return 0

    lax.fori_loop(1, ncols, gather_results, 0)

    full = parts[0]
    for src in range(1, ncols):
        full = full + parts[src]
    lane = lax.broadcasted_iota(jnp.int32, (1, tok), 1)
    query_rms = jnp.sqrt(full[3:5] / (ff * d_model) + epsilon)
    act_rms = jnp.sqrt(full[2:3] / ff + epsilon)
    grad_rms = jnp.sqrt(jnp.sum(gsq[...].T, axis=0, keepdims=True) / d_model + epsilon)
    positions = me * tok + lane
    seq_ids = lax.div(positions, LEN)
    limit = jnp.zeros((1, tok), jnp.int32)
    for q in range(seqs):
        limit = jnp.where(seq_ids == q, lens[q], limit)
    keep = lax.rem(positions, LEN) < limit
    influence = full[0:2] / (query_rms * act_rms * grad_rms * math.sqrt(ff * d_model))
    out[...] = jnp.where(keep, influence, 0.0)


def fused(ncols, activations, out_grads, queries, lengths):
    tok, d_model = out_grads.shape
    nq, ff_dev, _ = queries.shape
    pairs = ncols // 2
    sizes = (ncols, ff_dev * ncols, d_model, lengths.shape[0])
    tokens = ncols * tok
    dma = pltpu.SemaphoreType.DMA
    return pl.pallas_call(
        functools.partial(kernel, sizes),
        out_shape=jax.ShapeDtypeStruct((nq, tok), jnp.float32),
        in_specs=[pl.BlockSpec(memory_space=pl.ANY)] * 3 + [pl.BlockSpec(memory_space=pltpu.SMEM)],
        out_specs=pl.BlockSpec(memory_space=pltpu.VMEM),
        scratch_shapes=[
            pltpu.VMEM((pairs, 2, SUBS, tok, d_model // SUBS), jnp.bfloat16),
            pltpu.VMEM((pairs, 2 * tok, ff_dev), jnp.bfloat16),
            pltpu.VMEM((pairs, ff_dev, 2 * tok), jnp.float32),
            pltpu.VMEM((nq, ff_dev, d_model), jnp.bfloat16),
            pltpu.VMEM((pairs, nq, 8, 2 * tok), jnp.float32),
            pltpu.VMEM((pairs, 8, 2 * tok), jnp.float32),
            pltpu.VMEM((8, 2 * tok), jnp.float32),
            pltpu.VMEM((tok, LANES), jnp.float32),
            pltpu.VMEM((pairs, 2, 8, tok), jnp.float32),
            pltpu.VMEM((ncols, 8, tok), jnp.float32),
            dma((ncols, SUBS)), dma((8,)), dma((14,)), dma((14,)), dma((pairs, SUBS)),
            dma((pairs, 2)), dma((ncols,)), dma((3 + SUBS,)),
        ],
        compiler_params=pltpu.CompilerParams(
            collective_id=0, has_side_effects=True, vmem_limit_bytes=54 * 2**20),
        cost_estimate=pl.CostEstimate(
            flops=2 * nq * tokens * ff_dev * d_model, transcendentals=0,
            bytes_accessed=2 * (nq * ff_dev * d_model + tokens * ff_dev + tok * d_model)),
    )(out_grads, activations.reshape(pairs, 2 * tok, ff_dev), queries, lengths)


def local(activations, out_grads, queries, lengths):
    tok_dev, d_model = out_grads.shape
    query_sq = jnp.sum(jnp.square(queries.astype(jnp.float32)), axis=(1, 2))
    gathered = lax.all_gather(out_grads, "cols", axis=0, tiled=True)
    projected = jnp.einsum("rd,qfd->qrf", gathered, queries, preferred_element_type=jnp.float32)
    partials = jnp.sum(projected * activations.astype(jnp.float32)[None], axis=2)
    act_sq = jnp.sum(jnp.square(activations.astype(jnp.float32)), axis=1)[None, :]
    own_first = lax.axis_index("cols") * tok_dev
    total_scores, total_act, query_total = lax.psum((partials, act_sq, query_sq), "cols")
    own_scores = lax.dynamic_slice_in_dim(total_scores, own_first, tok_dev, 1)
    own_act = lax.dynamic_slice_in_dim(total_act, own_first, tok_dev, 1)
    ff = queries.shape[1] * lax.axis_size("cols")
    query_rms = jnp.sqrt(query_total / (ff * d_model) + epsilon)
    act_rms = jnp.sqrt(own_act[0] / ff + epsilon)
    grad_rms = jnp.sqrt(jnp.sum(jnp.square(out_grads.astype(jnp.float32)), axis=1) / d_model + epsilon)
    positions = own_first + jnp.arange(tok_dev, dtype=jnp.int32)
    seq_ids = positions // LEN
    owner_match = seq_ids[:, None] == jnp.arange(lengths.shape[0], dtype=jnp.int32)[None, :]
    seq_limit = jnp.sum(jnp.where(owner_match, lengths[None, :], 0), axis=1)
    keep_mask = positions % LEN < seq_limit
    denominator = query_rms[:, None] * act_rms[None, :] * grad_rms[None, :] * math.sqrt(ff * d_model)
    return jnp.where(keep_mask[None, :], own_scores / denominator, jnp.float32(0.0))


def solution(mesh):
    in_specs = (
        P("parts", "cols"),
        P(("parts", "cols"), None),
        P("parts", "cols", None),
        P("parts"),
    )
    out_specs = P(None, ("parts", "cols"))
    ncols = mesh.shape["cols"]
    body = functools.partial(fused, ncols) if ncols == 16 else local
    return jax.shard_map(body, mesh=mesh, in_specs=in_specs, out_specs=out_specs, check_vma=False)
```

time: 103 us -> 98.6 us (0.957)
  Pallas kernels: 102 us -> 97.2 us
    pallas_call x1, Pallas kernels: 102 us -> 97.2 us  [fused(): pl.pallas_call(functools.partial(kernel, sizes), out_shape=jax.ShapeDtype...]
where the time goes in v2:
time: 98.6 us; the launch traced here: 98.4 us
  Pallas kernels  97.2 us (99%)
  local copies, waits for them, and re-layouts  1.24 us (1%)
    pallas_call x1, Pallas kernels, fused(): pl.pallas_call(functools.partial(kernel, sizes), out_shape=jax.ShapeDtype...  97.2 us

profile of v2, /device:TPU:0, one launch (start us, length us, event | category | flops | bytes accessed | tf_op | source)
XLA Modules:
  0.0 98.4 jit_solution(2764450963451585727)
XLA Ops:
  0.0 97.2 %shard_map.46 = f32[2,128]{1,0:T(2,128)} custom-call(bf16[128,4096]{1,0:T(8,128)(2,1)} %og.1, bf16[8,256,896]{2,1,0:T(8,128)(2,1)} %bitcast.1, bf16[2,896,4096]{2,1,0:T(8,128)(2,1)} %qry.1, s32[2]{0:T(128)} %lens.1), custom_call_target="tpu_custom_call" | custom-call | flops 30064771072 | bytes 19398656 | tf_op jit(solution)/shard_map/pallas_call | solution.py:321
  97.2 1.2 %copy.6 = f32[2,128]{1,0:T(2,128)} copy(f32[2,128]{1,0:T(2,128)} %shard_map.46) | data formatting | bytes 2048

commit v3 on v2

--- a/solution.py
+++ b/solution.py
@@ -59,12 +59,17 @@
 
     barrier = pltpu.get_barrier_semaphore()
 
-    def greet(k, _):
-        pl.semaphore_signal(barrier, inc=1, device_id={"cols": lax.rem(me + k, ncols)}, device_id_type=MESH)
-        return 0
-
-    lax.fori_loop(1, ncols, greet, 0)
-    pl.semaphore_wait(barrier, ncols - 1)
+    def greet(target):
+        pl.semaphore_signal(barrier, inc=1, device_id={"cols": target}, device_id_type=MESH)
+
+    for target in (sib, ydev, indev):
+        greet(target)
+
+    @pl.when(mid)
+    def _():
+        greet(outdev)
+
+    pl.semaphore_wait(barrier, 3 + m)
 
     for s in range(SUBS):
         copy(mine(s), own, s, ydev, s_y.at[s]).start()
@@ -141,6 +146,22 @@
     def has_outer(u):
         return jnp.logical_and(mid, u < 6)
 
+    def settle(sem):
+        copy(mine(0), own, 0, sib, sem).wait_send()
+
+    def settle_links(k, _):
+        settle(s_y.at[k])
+
+        @pl.when(mid)
+        def _():
+            settle(s_out.at[k])
+
+        @pl.when(k < jnp.where(edge, 6, 8))
+        def _():
+            settle(s_in.at[k])
+
+        return 0
+
     def finish(p):
         tile = qtile[...]
         for k, value in enumerate((acc[p, 0], acc[p, 1], asq[p])):
@@ -172,6 +193,11 @@
             lhs = Q[q, :, pl.ds(pl.multiple_of(s * width, width), width)]
             pr = lax.dot_general(lhs, rhs, (((1,), (1,)), ((), ())), preferred_element_type=jnp.float32)
             acc[p, q] += jnp.sum((pr * AT[p]).reshape(ff_dev // 8, 8, 2 * tok), axis=0)
+
+            @pl.when(q == 1)
+            def _():
+                settle(s_sib.at[p, s])
+
             return 0
 
         lax.fori_loop(0, 2 * count, one, 0)
@@ -205,6 +231,10 @@
 
         lax.fori_loop(0, 3, task, 0)
 
+        @pl.when(jnp.logical_and(u >= 4, u < 14))
+        def _():
+            settle_links(u - 4, 0)
+
         @pl.when(has_inner(u))
         def _():
             p, s = inner_chunk(u)
@@ -257,30 +287,7 @@
 
     lax.fori_loop(0, 15, step, 0)
 
-    def settle(sem):
-        copy(mine(0), own, 0, sib, sem).wait_send()
-
-    def settle_links(k, _):
-        settle(s_y.at[k])
-
-        @pl.when(mid)
-        def _():
-            settle(s_out.at[k])
-
-        @pl.when(k < jnp.where(edge, 6, 8))
-        def _():
-            settle(s_in.at[k])
-
-        return 0
-
-    lax.fori_loop(0, 14, settle_links, 0)
-
-    def settle_sib(p, _):
-        for s in range(SUBS):
-            settle(s_sib.at[p, s])
-        return 0
-
-    lax.fori_loop(0, pairs, settle_sib, 0)
+    lax.fori_loop(10, 14, settle_links, 0)
 
     def gather_results(k, _):
         src = lax.rem(me + k, ncols)

time: 98.6 us -> 97.9 us (level)
  no operation moved by 1% of the time
where the time goes in v3:
time: 97.9 us; the launch traced here: 97.7 us
  Pallas kernels  96.5 us (99%)
  local copies, waits for them, and re-layouts  1.24 us (1%)
    pallas_call x1, Pallas kernels, fused(): pl.pallas_call(functools.partial(kernel, sizes), out_shape=jax.ShapeDtype...  96.5 us

profile of v3, /device:TPU:0, one launch (start us, length us, event | category | flops | bytes accessed | tf_op | source)
XLA Modules:
  0.0 97.7 jit_solution(16750920543002256785)
XLA Ops:
  0.0 96.5 %shard_map.46 = f32[2,128]{1,0:T(2,128)} custom-call(bf16[128,4096]{1,0:T(8,128)(2,1)} %og.1, bf16[8,256,896]{2,1,0:T(8,128)(2,1)} %bitcast.1, bf16[2,896,4096]{2,1,0:T(8,128)(2,1)} %qry.1, s32[2]{0:T(128)} %lens.1), custom_call_target="tpu_custom_call" | custom-call | flops 30064771072 | bytes 19398656 | tf_op jit(solution)/shard_map/pallas_call | solution.py:328
  96.5 1.2 %copy.6 = f32[2,128]{1,0:T(2,128)} copy(f32[2,128]{1,0:T(2,128)} %shard_map.46) | data formatting | bytes 2048
